TPU v7x, 32 devices: a whole 2x2x4 slice. The times are simulated.
32 devices in a mesh: parts: 2 (over y), dp: 8 (over z, x), tp: 2 (over core).
Axes of the slice: x: 2, y: 2, z: 4, core: 2. Of those that a mesh axis runs over, the one named last changes fastest.
Arguments:
- cache_keys: bfloat16 [256, 256, 512], P(('parts', 'dp'), None, 'tp'), parts along dimension 0, may hold values from -6 to 6
- cache_values: bfloat16 [256, 256, 512], P(('parts', 'dp'), None, 'tp'), parts along dimension 0, may hold values from -6 to 6
- lengths: int32 [256], P(('parts', 'dp')), parts along dimension 0, may hold values from 1 to 2, as said below
- move_to: int32 [256], P(('parts', 'dp')), parts along dimension 0, may hold values from 0 to 127, as said below
- queries: bfloat16 [256, 2, 4096], P(('parts', 'dp'), None, 'tp'), parts along dimension 0, may hold values from -150 to 150
- new_keys: bfloat16 [256, 2, 512], P(('parts', 'dp'), None, 'tp'), parts along dimension 0, may hold values from -8 to 8
- new_values: bfloat16 [256, 2, 512], P(('parts', 'dp'), None, 'tp'), parts along dimension 0, may hold values from -6 to 6
- out_weight: bfloat16 [4096, 5120], P('tp', 'dp'), may hold values from -0.09375 to 0.09375
Outputs:
- hidden: bfloat16 [256, 2, 5120], P(('parts', 'dp')), parts along dimension 0
There are 2 independent parts, one for each index of `parts`. A program takes and returns all parts, laid end to end along the dimension named above; an argument that names none is the same for every part. Nothing has to cross between parts.
Inputs may be any that keep to these rules, and one draw needn't show every extreme that they name: `lengths`: at least one row has 2 blocks and at least one has 1. `move_to`: a permutation of the 128 slots (slot = group * 16 + index in the group, with 8 groups); in every group the same 7 indices leave and the others stay in place; the k-th of the leaving indices (k = 1 to 7, which index is which k is drawn) goes, at the same index, to the group 1 + (k - 1) * max(1, 1) further on, counted cyclically.
All inputs are finite; a program needn't handle non-finite values.
Results may differ from a plain program's by a relative error of at most 0.0057.
Values may be sent and summed in bfloat16 or wider, within the bound.
A program may use at most 64 MiB of HBM per device.

v0:
```python
import math

import jax
import jax.numpy as jnp
from jax import lax
from jax.sharding import PartitionSpec as P

KVH = 4
HD = 128
BLK = 128


def shifted(shard, axis, by):
    count = lax.axis_size(axis)
    return lax.ppermute(shard, axis, [(i, (i + by) % count) for i in range(count)])


def attend(queries, new_keys, new_values, keys, values, row_lengths, heads_kv):
    row_count, step_count, query_width = queries.shape
    span_len = keys.shape[1]
    group_size = query_width // (heads_kv * HD)
    score_scale = 1.0 / math.sqrt(HD)
    query = queries.reshape(row_count, step_count, heads_kv, group_size, HD)
    key_block = keys.reshape(row_count, span_len, heads_kv, HD)
    value_block = values.reshape(row_count, span_len, heads_kv, HD)
    fresh_keys = new_keys.reshape(row_count, step_count, heads_kv, HD)
    fresh_values = new_values.reshape(row_count, step_count, heads_kv, HD)
    cache_scores = (
        jnp.einsum("bskgd,bpkd->bskgp", query, key_block, preferred_element_type=jnp.float32)
        * score_scale
    )
    fresh_scores = (
        jnp.einsum("bskgd,bukd->bskgu", query, fresh_keys, preferred_element_type=jnp.float32)
        * score_scale
    )
    visible = jnp.arange(span_len)[None, :] < (row_lengths * BLK)[:, None]
    causal = jnp.arange(step_count)[None, :] <= jnp.arange(step_count)[:, None]
    cache_scores = jnp.where(visible[:, None, None, None, :], cache_scores, -jnp.inf)
    fresh_scores = jnp.where(causal[None, :, None, None, :], fresh_scores, -jnp.inf)
    top_score = jnp.maximum(cache_scores.max(axis=-1), fresh_scores.max(axis=-1))[..., None]
    cache_exp = jnp.exp(cache_scores - top_score)
    fresh_exp = jnp.exp(fresh_scores - top_score)
    sum_exp = cache_exp.sum(axis=-1, keepdims=True) + fresh_exp.sum(axis=-1, keepdims=True)
    cache_weight = (cache_exp / sum_exp).astype(jnp.bfloat16)
    fresh_weight = (fresh_exp / sum_exp).astype(jnp.bfloat16)
    mixed = jnp.einsum(
        "bskgp,bpkd->bskgd", cache_weight, value_block, preferred_element_type=jnp.float32
    )
    mixed = mixed + jnp.einsum(
        "bskgu,bukd->bskgd", fresh_weight, fresh_values, preferred_element_type=jnp.float32
    )
    return mixed.astype(jnp.bfloat16).reshape(row_count, step_count, query_width)


def pick_row(array, index):
    return lax.dynamic_index_in_dim(array, index, 0, keepdims=True)


def place_row(array, row, index):
    return lax.dynamic_update_slice_in_dim(array, row, index, 0)


def ship_cache(payload, offset):
    return shifted((payload[0], payload[1]), "dp", offset)


def local(cache_keys, cache_values, lengths, move_to, queries, new_keys, new_values, out_weight):
    group_count = lax.axis_size("dp")
    my_group = lax.axis_index("dp")
    row_count = lengths.shape[0]
    heads_kv = KVH // lax.axis_size("tp")
    moves = min(row_count // 2, group_count - 1)
    stride = max(1, group_count // (moves + 1))
    all_moves, all_lengths = (
        lax.all_gather(move_to, "dp", axis=0, tiled=True),
        lax.all_gather(lengths, "dp", axis=0, tiled=True),
    )
    slot_ids = jnp.arange(all_moves.shape[0], dtype=jnp.int32)
    local_ids = jnp.arange(row_count, dtype=jnp.int32)
    my_slots = my_group * row_count + local_ids
    arrives = all_moves[None, :] == my_slots[:, None]
    source_slot = jnp.sum(jnp.where(arrives, slot_ids[None, :], 0), axis=1)
    source_group = source_slot // row_count
    dest_group = move_to // row_count
    out_list = []
    in_list = []
    for step in range(moves):
        offset = 1 + step * stride
        to_group = (my_group + offset) % group_count
        from_group = (my_group + group_count - offset) % group_count
        out_list.append(jnp.sum(jnp.where(dest_group == to_group, local_ids, 0)))
        in_list.append(jnp.sum(jnp.where(source_group == from_group, local_ids, 0)))
    moved_keys, moved_values = (cache_keys, cache_values)
    for step in range(moves):
        offset = 1 + step * stride
        got_keys, got_values = ship_cache(
            (pick_row(cache_keys, out_list[step]), pick_row(cache_values, out_list[step])), offset
        )
        moved_keys = place_row(moved_keys, got_keys, in_list[step])
        moved_values = place_row(moved_values, got_values, in_list[step])
    moved_lengths = jnp.sum(jnp.where(arrives, all_lengths[None, :], 0), axis=1)
    attended = attend(
        queries, new_keys, new_values, moved_keys, moved_values, moved_lengths, heads_kv
    )
    flat_rows = attended.reshape(-1, attended.shape[-1])
    partial_sums = jnp.dot(
        lax.all_gather(flat_rows, "dp", axis=0, tiled=True),
        out_weight,
        preferred_element_type=jnp.float32,
    )
    summed = lax.psum(partial_sums, "tp").astype(jnp.bfloat16)
    summed = lax.all_to_all(summed, "dp", split_axis=0, concat_axis=1, tiled=True)
    return summed.reshape(attended.shape[0], attended.shape[1], -1)


def solution(mesh):
    placed = (
        P(("parts", "dp"), None, "tp"),
        P(("parts", "dp"), None, "tp"),
        P(("parts", "dp")),
        P(("parts", "dp")),
        P(("parts", "dp"), None, "tp"),
        P(("parts", "dp"), None, "tp"),
        P(("parts", "dp"), None, "tp"),
        P("tp", "dp"),
    )
    return jax.shard_map(
        local, mesh=mesh, in_specs=placed, out_specs=P(("parts", "dp"), None, None), check_vma=False
    )
```

profile of v0, /device:TPU:1, one launch (start us, length us, event | category | flops | bytes accessed | tf_op | source)
XLA Modules:
  0.0 192.8 jit_solution(6405769611158128526)
XLA Ops:
  6.5 3.2 %copy.122 = bf16[16,256,256]{2,1,0:T(8,128)(2,1)} copy(bf16[16,256,256]{2,1,0:T(8,128)(2,1)} %param.9) | data formatting | bytes 4194304
  9.8 0.0 copy-start.2
  9.8 0.0 copy-start.8
  9.8 1.4 copy.121
  11.2 0.8 fusion.48
  13.9 0.9 constant_dynamic-slice_fusion.13
  14.8 2.1 %collective-permute-start = (bf16[1,256,256]{2,1,0:T(8,128)(2,1)S(1)}, bf16[1,256,256]{2,1,0:T(8,128)(2,1)S(1)}, u32[]{:S(2)}, u32[]{:S(2)}) collective-permute-start(bf16[1,256,256]{2,1,0:T(8,128)(2,1)S(1)} %constant_dynamic-slice_fusion.13), channel_id=1, source_target_pairs={{0,2},{2,4},{4,6},{6,8},{8,10},{10,12},{12,14},{14,0},{1,3},{3,5},... | collective-permute-start | bytes 393224 | tf_op jit(solution)/shard_map/ppermute | solution.py:15
  16.9 0.9 constant_dynamic-slice_fusion.6
  17.8 1.3 collective-permute-start.7
  19.1 0.6 dynamic-slice
  20.4 0.2 dynamic-update-slice
  20.6 0.2 dynamic-update-slice.1
  20.9 8.4 %all-reduce.2 = (s32[128]{0:T(128)S(1)}, s32[128]{0:T(128)S(1)}) all-reduce(s32[128]{0:T(128)S(1)} %dynamic-update-slice.1, s32[128]{0:T(128)S(1)} %dynamic-update-slice), channel_id=1, replica_groups=mesh['parts'=2,'dp'=8,'tp'=2] {'dp'}, use_global_device_ids=true, to_apply=%add.1 | all-reduce | flops 256 | bytes 2048
  29.3 0.2 fusion.35
  29.5 0.8 fusion.49
  38.9 0.1 reshape.73
  39.0 0.0 copy-start.3
  43.3 1.9 %fusion.51 = (f32[16,2,2,8]{3,1,2,0:T(2,128)}, f32[16,2,2,8,2]{3,4,1,2,0:T(2,128)}) fusion(bf16[16,2,2,8,128]{4,3,2,1,0:T(8,128)(2,1)S(1)} %reshape.73, bf16[16,2,256]{2,1,0:T(2,128)(2,1)S(1)} %copy-done.8, pred[2,2]{1,0:T(4,128)(4,1)S(1)} %iota_compare_fusion.1), kind=kOutput, calls=%fused_computation.101 | convolution fusion | flops 264704 | bytes 153604 | tf_op jit(solution)/shard_map/bskgd,bukd->bskgu/dot_general | solution.py:33
  45.3 0.0 collective-permute-done
  45.3 2.0 %constant_dynamic-slice_fusion.7 = (bf16[1,256,256]{2,1,0:T(8,128)(2,1)S(1)}, bf16[1,256,256]{2,1,0:T(8,128)(2,1)S(1)}, bf16[1,256,256]{2,1,0:T(8,128)(2,1)}, bf...) fusion(bf16[16,256,256]{2,1,0:T(8,128)(2,1)} %copy.122, ...), kind=kLoop, calls=%fused_computation.48 | loop fusion | bytes 1835036 | tf_op jit(solution)/shard_map/jit(dynamic_index_in_dim)/dynamic_slice | solution.py:56
  47.3 1.2 collective-permute-start.1
  48.5 0.0 collective-permute-done.7
  48.5 2.0 %constant_dynamic-slice_fusion = (bf16[1,256,256]{2,1,0:T(8,128)(2,1)S(1)}, bf16[1,256,256]{2,1,0:T(8,128)(2,1)S(1)}, bf16[1,256,256]{2,1,0:T(8,128)(2,1)}, bf16...) fusion(bf16[16,256,256]{2,1,0:T(8,128)(2,1)} %copy.121, ...), kind=kLoop, calls=%fused_computation.34 | loop fusion | bytes 1835036 | tf_op jit(solution)/shard_map/jit(dynamic_index_in_dim)/dynamic_slice | solution.py:56
  50.5 0.2 collective-permute-start.8
  50.7 0.1 iota_compare_fusion
  62.2 0.5 collective-permute-start.2
  62.7 3.3 %collective-permute-start.3 = (bf16[1,256,256]{2,1,0:T(8,128)(2,1)}, bf16[1,256,256]{2,1,0:T(8,128)(2,1)S(1)}, u32[]{:S(2)}, u32[]{:S(2)}) collective-permute-start(bf16[1,256,256]{2,1,0:T(8,128)(2,1)} %get-tuple-element.25), channel_id=1, source_target_pairs={{0,8},{2,10},{4,12},{6,14},{8,0},{10,2},{12,4},{14,6},{1,9},{3,11}... | collective-permute-start | bytes 393224 | tf_op jit(solution)/shard_map/ppermute | solution.py:15
  65.9 1.8 collective-permute-start.4
  67.7 0.0 collective-permute-done.1
  67.7 0.9 collective-permute-start.5
  68.6 1.6 constant_dynamic-update-slice_fusion.12
  70.2 0.8 collective-permute-start.9
  71.0 0.7 constant_dynamic-update-slice_fusion.5
  71.7 2.7 %collective-permute-start.6 = (bf16[1,256,256]{2,1,0:T(8,128)(2,1)S(1)}, bf16[1,256,256]{2,1,0:T(8,128)(2,1)S(1)}, u32[]{:S(2)}, u32[]{:S(2)}) collective-permute-start(bf16[1,256,256]{2,1,0:T(8,128)(2,1)S(1)} %get-tuple-element.23), channel_id=1, source_target_pairs={{0,14},{2,0},{4,2},{6,4},{8,6},{10,8},{12,10},{14,12},{1,15},{3,1}... | collective-permute-start | bytes 393224 | tf_op jit(solution)/shard_map/ppermute | solution.py:15
  74.4 0.7 constant_dynamic-update-slice_fusion.11
  75.1 12.2 %collective-permute-done.9 = bf16[1,256,256]{2,1,0:T(8,128)(2,1)S(1)} collective-permute-done((bf16[1,256,256]{2,1,0:T(8,128)(2,1)}, bf16[1,256,256]{2,1,0:T(8,128)(2,1)S(1)}, u32[]{:S(2)}, u32[]{:S(2)}) %collective-permute-start.9) | collective-permute-done | bytes 131104 | tf_op jit(solution)/shard_map/ppermute | solution.py:15
  87.3 0.7 constant_dynamic-update-slice_fusion.4
  87.9 0.7 collective-permute-start.11
  88.7 0.7 constant_dynamic-update-slice_fusion.10
  89.3 2.9 %collective-permute-done.10 = bf16[1,256,256]{2,1,0:T(8,128)(2,1)S(1)} collective-permute-done((bf16[1,256,256]{2,1,0:T(8,128)(2,1)}, bf16[1,256,256]{2,1,0:T(8,128)(2,1)S(1)}, u32[]{:S(2)}, u32[]{:S(2)}) %collective-permute-start.10) | collective-permute-done | bytes 131104 | tf_op jit(solution)/shard_map/ppermute | solution.py:15
  92.2 5.8 %collective-permute-start.12 = (bf16[1,256,256]{2,1,0:T(8,128)(2,1)S(1)}, bf16[1,256,256]{2,1,0:T(8,128)(2,1)S(1)}, u32[]{:S(2)}, u32[]{:S(2)}) collective-permute-start(bf16[1,256,256]{2,1,0:T(8,128)(2,1)S(1)} %get-tuple-element.36), channel_id=1, source_target_pairs={{0,12},{2,14},{4,0},{6,2},{8,4},{10,6},{12,8},{14,10},{1,13},{3,15... | collective-permute-start | bytes 393224 | tf_op jit(solution)/shard_map/ppermute | solution.py:15
  98.0 0.7 constant_dynamic-update-slice_fusion.3
  98.7 0.7 constant_dynamic-update-slice_fusion.9
  99.3 0.7 constant_dynamic-update-slice_fusion.2
  100.0 0.7 constant_dynamic-update-slice_fusion.8
  100.6 0.7 constant_dynamic-update-slice_fusion.1
  101.3 1.2 collective-permute-done.13
  102.5 0.7 constant_dynamic-update-slice_fusion
  103.2 4.0 %reshape.72 = bf16[16,256,2,128]{3,2,1,0:T(2,128)(2,1)} reshape(bf16[16,256,256]{2,1,0:T(8,128)(2,1)} %get-tuple-element.41) | data formatting | bytes 4194304 | tf_op jit(solution)/shard_map/reshape | solution.py:24
  107.2 2.4 %fusion.50 = (f32[16,2,2,8]{3,1,2,0:T(2,128)S(1)}, f32[16,2,2,8,256]{4,3,1,2,0:T(8,128)S(1)}) fusion(bf16[16,2,2,8,128]{4,3,2,1,0:T(8,128)(2,1)S(1)} %copy-done.4, bf16[16,256,2,128,1]{3,2,1,0,4:T(2,128)(2,1)} %bitcast.40, pred[16,256]{1,0:T(8,128)(4,1)S(1)} %iota_compare_fusion), kind=kOutput, calls=%fused_computation.100 | convolution fusion | flops 33947136 | bytes 2758656 | tf_op jit(solution)/shard_map/bskgd,bpkd->bskgp/dot_general | solution.py:29
  109.6 0.1 fusion.29
  109.8 0.3 fusion.24
  110.1 0.0 copy-start.9
  110.1 4.0 %reshape.71 = bf16[16,256,2,128]{3,2,1,0:T(2,128)(2,1)} reshape(bf16[16,256,256]{2,1,0:T(8,128)(2,1)} %get-tuple-element.42) | data formatting | bytes 4194304 | tf_op jit(solution)/shard_map/reshape | solution.py:25
  114.1 0.3 convolution_bitcast_fusion
  114.4 2.0 %fusion.19 = bf16[16,2,2,8,128]{4,3,1,2,0:T(8,128)(2,1)S(1)} fusion(f32[16,2,2,8,128]{4,3,1,2,0:T(8,128)S(1)} %convolution_bitcast_fusion, bf16[16,256,2,128,1]{3,2,1,0,4:T(2,128)(2,1)} %bitcast.39, f32[16,2,2,8,256]{4,3,1,2,0:T(8,128)S(1)} %get-tuple-element.38, f32[16,2,2,8]{3,1,2,0:T(2,128)S(1)} %add.181, f32[16,2,2,8]{3,1,2,0:T(2,128)S(1)} %max.7), kind=kOutput, calls=%fused_computation.10 | convolution fusion | flops 34078720 | bytes 3018752 | tf_op jit(solution)/shard_map/bskgp,bpkd->bskgd/dot_general | solution.py:46
  116.4 0.7 reshape_reshape.3
  117.1 0.0 all-gather.2.cloned.1.call-update
  117.2 44.6 %all-gather.2.cloned.1.call-done = bf16[256,2048]{1,0:T(8,128)(2,1)} async-done(((bf16[32,2048]{1,0:T(8,128)(2,1)}), bf16[256,2048]{1,0:T(8,128)(2,1)}) %all-gather.2.cloned.1.call-update) | async-done | bytes 1048592 | tf_op jit(solution)/shard_map/all_gather | solution.py:107
  161.8 3.1 %fusion.52 = f32[256,640]{1,0:T(8,128)} fusion(bf16[256,2048]{1,0:T(8,128)(2,1)} %all-gather.2.cloned.1.call-done, bf16[2048,640]{1,0:T(8,128)(2,1)S(1)} %copy-done), kind=kOutput, calls=%fused_computation.102 | convolution fusion | flops 671088640 | bytes 4325376 | tf_op jit(solution)/shard_map/dot_general | solution.py:106
  164.9 7.5 %all-reduce.4 = bf16[256,640]{1,0:T(8,128)(2,1)S(1)} all-reduce(f32[256,640]{1,0:T(8,128)} %fusion.52), channel_id=1, replica_groups=mesh['parts'=2,'dp'=8,'tp'=2] {'tp'}, use_global_device_ids=true, to_apply=%region_20.21 | all-reduce | flops 163840 | bytes 983040 | tf_op jit(solution)/shard_map/psum | solution.py:111
  172.3 12.7 %all_to_all.16 = bf16[8,32,640]{2,1,0:T(8,128)(2,1)S(1)} all-to-all(bf16[8,32,640]{2,1,0:T(8,128)(2,1)S(1)} %bitcast.42), channel_id=1, replica_groups=mesh['parts'=2,'dp'=8,'tp'=2] {'dp'}, dimensions={0} | all-to-all | bytes 655360 | tf_op jit(solution)/shard_map/all_to_all | solution.py:112
  185.0 0.1 copy.31
  185.1 0.8 reshape.76
  (39 shorter events, 0.1 us)
Async XLA Ops:
  6.5 155.3 %copy-start = (bf16[2048,640]{1,0:T(8,128)(2,1)S(1)}, bf16[2048,640]{1,0:T(8,128)(2,1)}, u32[]{:S(2)}) copy-start(bf16[2048,640]{1,0:T(8,128)(2,1)} %param.15) | copy-start | bytes 7864324
  6.5 155.3 %all-gather.2.cloned.1.call-start = ((), (), s32[]{:S(2)}) async-start(), calls=%async_computation.1 | async-start | bytes 1179648 | tf_op jit(solution)/shard_map/all_gather | solution.py:107
  6.5 3.2 %copy-start.1 = (bf16[16,256,256]{2,1,0:T(8,128)(2,1)S(1)}, bf16[16,256,256]{2,1,0:T(8,128)(2,1)}, u32[]{:S(2)}) copy-start(bf16[16,256,256]{2,1,0:T(8,128)(2,1)} %param.8) | copy-start | bytes 6291460
  9.8 1.4 copy-start.7
  9.8 9.4 %copy-start.11 = (u32[32]{0:T(128)S(1)}, u32[32]{0:T(128)}, u32[]{:S(2)}) copy-start(u32[32]{0:T(128)} %constant.161) | copy-start | bytes 388
  9.8 10.9 %copy-start.10 = (s32[16]{0:T(128)S(1)}, s32[16]{0:T(128)}, u32[]{:S(2)}) copy-start(s32[16]{0:T(128)} %param.10) | copy-start | bytes 196
  9.8 29.1 %copy-start.2 = (bf16[16,2,2048]{2,1,0:T(2,128)(2,1)S(1)}, bf16[16,2,2048]{2,1,0:T(2,128)(2,1)}, u32[]{:S(2)}) copy-start(bf16[16,2,2048]{2,1,0:T(2,128)(2,1)} %param.12) | copy-start | bytes 393220
  9.8 33.5 %copy-start.8 = (bf16[16,2,256]{2,1,0:T(2,128)(2,1)S(1)}, bf16[16,2,256]{2,1,0:T(2,128)(2,1)}, u32[]{:S(2)}) copy-start(bf16[16,2,256]{2,1,0:T(2,128)(2,1)} %param.13) | copy-start | bytes 49156
  14.8 30.5 %collective-permute-start = (bf16[1,256,256]{2,1,0:T(8,128)(2,1)S(1)}, bf16[1,256,256]{2,1,0:T(8,128)(2,1)S(1)}, u32[]{:S(2)}, u32[]{:S(2)}) collective-permute-start(bf16[1,256,256]{2,1,0:T(8,128)(2,1)S(1)} %constant_dynamic-slice_fusion.13), channel_id=1, source_target_pairs={{0,2},{2,4},{4,6},{6,8},{8,10},{10,12},{12,14},{14,0},{1,3},{3,5},... | collective-permute-start | bytes 393224 | tf_op jit(solution)/shard_map/ppermute | solution.py:15
  17.8 30.7 %collective-permute-start.7 = (bf16[1,256,256]{2,1,0:T(8,128)(2,1)S(1)}, bf16[1,256,256]{2,1,0:T(8,128)(2,1)S(1)}, u32[]{:S(2)}, u32[]{:S(2)}) collective-permute-start(bf16[1,256,256]{2,1,0:T(8,128)(2,1)S(1)} %constant_dynamic-slice_fusion.6), channel_id=1, source_target_pairs={{0,2},{2,4},{4,6},{6,8},{8,10},{10,12},{12,14},{14,0},{1,3},{3,5},... | collective-permute-start | bytes 393224 | tf_op jit(solution)/shard_map/ppermute | solution.py:15
  39.0 6.3 %copy-start.3 = (bf16[16,2,2,8,128]{4,3,2,1,0:T(8,128)(2,1)}, bf16[16,2,2,8,128]{4,3,2,1,0:T(8,128)(2,1)S(1)}, u32[]{:S(2)}) copy-start(bf16[16,2,2,8,128]{4,3,2,1,0:T(8,128)(2,1)S(1)} %reshape.73) | copy-start | bytes 393220
  47.3 20.4 %collective-permute-start.1 = (bf16[1,256,256]{2,1,0:T(8,128)(2,1)}, bf16[1,256,256]{2,1,0:T(8,128)(2,1)}, u32[]{:S(2)}, u32[]{:S(2)}) collective-permute-start(bf16[1,256,256]{2,1,0:T(8,128)(2,1)} %get-tuple-element.27), channel_id=1, source_target_pairs={{0,4},{2,6},{4,8},{6,10},{8,12},{10,14},{12,0},{14,2},{1,5},{3,7},... | collective-permute-start | bytes 393224 | tf_op jit(solution)/shard_map/ppermute | solution.py:15
  50.5 19.7 %collective-permute-start.8 = (bf16[1,256,256]{2,1,0:T(8,128)(2,1)}, bf16[1,256,256]{2,1,0:T(8,128)(2,1)S(1)}, u32[]{:S(2)}, u32[]{:S(2)}) collective-permute-start(bf16[1,256,256]{2,1,0:T(8,128)(2,1)} %get-tuple-element.34), channel_id=1, source_target_pairs={{0,4},{2,6},{4,8},{6,10},{8,12},{10,14},{12,0},{14,2},{1,5},{3,7},... | collective-permute-start | bytes 393224 | tf_op jit(solution)/shard_map/ppermute | solution.py:15
  62.2 9.5 %collective-permute-start.2 = (bf16[1,256,256]{2,1,0:T(8,128)(2,1)}, bf16[1,256,256]{2,1,0:T(8,128)(2,1)S(1)}, u32[]{:S(2)}, u32[]{:S(2)}) collective-permute-start(bf16[1,256,256]{2,1,0:T(8,128)(2,1)} %get-tuple-element.26), channel_id=1, source_target_pairs={{0,6},{2,8},{4,10},{6,12},{8,14},{10,0},{12,2},{14,4},{1,7},{3,9},... | collective-permute-start | bytes 393224 | tf_op jit(solution)/shard_map/ppermute | solution.py:15
  62.7 25.2 %collective-permute-start.3 = (bf16[1,256,256]{2,1,0:T(8,128)(2,1)}, bf16[1,256,256]{2,1,0:T(8,128)(2,1)S(1)}, u32[]{:S(2)}, u32[]{:S(2)}) collective-permute-start(bf16[1,256,256]{2,1,0:T(8,128)(2,1)} %get-tuple-element.25), channel_id=1, source_target_pairs={{0,8},{2,10},{4,12},{6,14},{8,0},{10,2},{12,4},{14,6},{1,9},{3,11}... | collective-permute-start | bytes 393224 | tf_op jit(solution)/shard_map/ppermute | solution.py:15
  65.9 32.7 %collective-permute-start.4 = (bf16[1,256,256]{2,1,0:T(8,128)(2,1)S(1)}, bf16[1,256,256]{2,1,0:T(8,128)(2,1)S(1)}, u32[]{:S(2)}, u32[]{:S(2)}) collective-permute-start(bf16[1,256,256]{2,1,0:T(8,128)(2,1)S(1)} %get-tuple-element.24), channel_id=1, source_target_pairs={{0,10},{2,12},{4,14},{6,0},{8,2},{10,4},{12,6},{14,8},{1,11},{3,13... | collective-permute-start | bytes 393224 | tf_op jit(solution)/shard_map/ppermute | solution.py:15
  67.7 32.3 %collective-permute-start.5 = (bf16[1,256,256]{2,1,0:T(8,128)(2,1)S(1)}, bf16[1,256,256]{2,1,0:T(8,128)(2,1)S(1)}, u32[]{:S(2)}, u32[]{:S(2)}) collective-permute-start(bf16[1,256,256]{2,1,0:T(8,128)(2,1)S(1)} %get-tuple-element.29), channel_id=1, source_target_pairs={{0,12},{2,14},{4,0},{6,2},{8,4},{10,6},{12,8},{14,10},{1,13},{3,15... | collective-permute-start | bytes 393224 | tf_op jit(solution)/shard_map/ppermute | solution.py:15
  70.2 17.1 %collective-permute-start.9 = (bf16[1,256,256]{2,1,0:T(8,128)(2,1)}, bf16[1,256,256]{2,1,0:T(8,128)(2,1)S(1)}, u32[]{:S(2)}, u32[]{:S(2)}) collective-permute-start(bf16[1,256,256]{2,1,0:T(8,128)(2,1)} %get-tuple-element.33), channel_id=1, source_target_pairs={{0,6},{2,8},{4,10},{6,12},{8,14},{10,0},{12,2},{14,4},{1,7},{3,9},... | collective-permute-start | bytes 393224 | tf_op jit(solution)/shard_map/ppermute | solution.py:15
  71.7 29.6 %collective-permute-start.6 = (bf16[1,256,256]{2,1,0:T(8,128)(2,1)S(1)}, bf16[1,256,256]{2,1,0:T(8,128)(2,1)S(1)}, u32[]{:S(2)}, u32[]{:S(2)}) collective-permute-start(bf16[1,256,256]{2,1,0:T(8,128)(2,1)S(1)} %get-tuple-element.23), channel_id=1, source_target_pairs={{0,14},{2,0},{4,2},{6,4},{8,6},{10,8},{12,10},{14,12},{1,15},{3,1}... | collective-permute-start | bytes 393224 | tf_op jit(solution)/shard_map/ppermute | solution.py:15
  87.3 4.9 %collective-permute-start.10 = (bf16[1,256,256]{2,1,0:T(8,128)(2,1)}, bf16[1,256,256]{2,1,0:T(8,128)(2,1)S(1)}, u32[]{:S(2)}, u32[]{:S(2)}) collective-permute-start(bf16[1,256,256]{2,1,0:T(8,128)(2,1)} %get-tuple-element.32), channel_id=1, source_target_pairs={{0,8},{2,10},{4,12},{6,14},{8,0},{10,2},{12,4},{14,6},{1,9},{3,11}... | collective-permute-start | bytes 393224 | tf_op jit(solution)/shard_map/ppermute | solution.py:15
  87.9 11.4 %collective-permute-start.11 = (bf16[1,256,256]{2,1,0:T(8,128)(2,1)S(1)}, bf16[1,256,256]{2,1,0:T(8,128)(2,1)S(1)}, u32[]{:S(2)}, u32[]{:S(2)}) collective-permute-start(bf16[1,256,256]{2,1,0:T(8,128)(2,1)S(1)} %get-tuple-element.31), channel_id=1, source_target_pairs={{0,10},{2,12},{4,14},{6,0},{8,2},{10,4},{12,6},{14,8},{1,11},{3,13... | collective-permute-start | bytes 393224 | tf_op jit(solution)/shard_map/ppermute | solution.py:15
  92.2 8.4 %collective-permute-start.12 = (bf16[1,256,256]{2,1,0:T(8,128)(2,1)S(1)}, bf16[1,256,256]{2,1,0:T(8,128)(2,1)S(1)}, u32[]{:S(2)}, u32[]{:S(2)}) collective-permute-start(bf16[1,256,256]{2,1,0:T(8,128)(2,1)S(1)} %get-tuple-element.36), channel_id=1, source_target_pairs={{0,12},{2,14},{4,0},{6,2},{8,4},{10,6},{12,8},{14,10},{1,13},{3,15... | collective-permute-start | bytes 393224 | tf_op jit(solution)/shard_map/ppermute | solution.py:15
  98.7 3.8 %collective-permute-start.13 = (bf16[1,256,256]{2,1,0:T(8,128)(2,1)S(1)}, bf16[1,256,256]{2,1,0:T(8,128)(2,1)S(1)}, u32[]{:S(2)}, u32[]{:S(2)}) collective-permute-start(bf16[1,256,256]{2,1,0:T(8,128)(2,1)S(1)} %get-tuple-element.30), channel_id=1, source_target_pairs={{0,14},{2,0},{4,2},{6,4},{8,6},{10,8},{12,10},{14,12},{1,15},{3,1}... | collective-permute-start | bytes 393224 | tf_op jit(solution)/shard_map/ppermute | solution.py:15
  103.2 4.0 %copy-start.4 = (bf16[16,2,2,8,128]{4,3,2,1,0:T(8,128)(2,1)S(1)}, bf16[16,2,2,8,128]{4,3,2,1,0:T(8,128)(2,1)}, u32[]{:S(2)}) copy-start(bf16[16,2,2,8,128]{4,3,2,1,0:T(8,128)(2,1)} %copy-done.3) | copy-start | bytes 393220
  107.2 2.4 %copy-start.6 = (f32[16,2,2,8]{3,1,2,0:T(2,128)S(1)}, f32[16,2,2,8]{3,1,2,0:T(2,128)}, u32[]{:S(2)}) copy-start(f32[16,2,2,8]{3,1,2,0:T(2,128)} %get-tuple-element.39) | copy-start | bytes 6148
  107.2 2.4 %copy-start.5 = (f32[16,2,2,8,2]{3,4,1,2,0:T(2,128)S(1)}, f32[16,2,2,8,2]{3,4,1,2,0:T(2,128)}, u32[]{:S(2)}) copy-start(f32[16,2,2,8,2]{3,4,1,2,0:T(2,128)} %get-tuple-element.40) | copy-start | bytes 12292
  110.1 4.0 %copy-start.9 = (bf16[16,2,256]{2,1,0:T(2,128)(2,1)S(1)}, bf16[16,2,256]{2,1,0:T(2,128)(2,1)}, u32[]{:S(2)}) copy-start(bf16[16,2,256]{2,1,0:T(2,128)(2,1)} %param.14) | copy-start | bytes 49156
Sparse Core Ops, SparseCore 0:
  117.3 44.4 all-gather.1
where the time goes:
time: 196 us; the launch traced here: 193 us
  waiting for transfers between devices  60.9 us (31%)
  between operations  40.6 us (21%)
  local copies, waits for them, and re-layouts  29.5 us (15%)
  blocking collectives  28.6 us (15%)
  starting transfers between devices  21.2 us (11%)
  matrix products  9.67 us (5%)
  other arithmetic  2.3 us (1%)
    all_gather x1, waiting for transfers between devices, local(): lax.all_gather(flat_rows, 'dp', axis=0, tiled=True)  44.6 us
    ppermute x14, starting transfers between devices, shifted(): lax.ppermute(shard, axis, [(i, (i + by) % count) for i in range(count)])  21.2 us
    ppermute x14, waiting for transfers between devices, shifted(): lax.ppermute(shard, axis, [(i, (i + by) % count) for i in range(count)])  16.3 us
    all_to_all x1, blocking collectives, local(): lax.all_to_all(summed, 'dp', split_axis=0, concat_axis=1, tiled=True)  12.7 us
    unnamed x1, blocking collectives  8.41 us
    dynamic_update_slice x11, local copies, waits for them, and re-layouts, place_row(): return lax.dynamic_update_slice_in_dim(array, row, index, 0)  8.2 us
    psum x1, blocking collectives, local(): summed = lax.psum(partial_sums, 'tp').astype(jnp.bfloat16)  7.47 us
    dynamic_slice x4, local copies, waits for them, and re-layouts, pick_row(): return lax.dynamic_index_in_dim(array, index, 0, keepdims=True)  5.86 us
  transfers between devices with their start and end apart: 15, of which 4 were waited for; matrix products, arithmetic and copies ran while one was open for 9% of the time, Pallas kernels for 0%

commit v1 on v0

v1 whole, which is shorter than its diff:
```python
import functools
import math

import jax
import jax.numpy as jnp
from jax import lax
from jax.experimental import pallas as pl
from jax.experimental.pallas import tpu as pltpu
from jax.sharding import PartitionSpec as P

KVH = 4
HD = 128
BLK = 128
STEPS = 2
PAY = 48
MESH = pl.DeviceIdType.MESH


def attend_slot(pay, keys, values, length):
    query = pay[0:32].astype(jnp.float32)
    extra = pay[32:48].astype(jnp.float32)
    row = lax.broadcasted_iota(jnp.int32, (32, HD), 0)
    first_kv = (row // 8) % 2 == 0
    zero = jnp.zeros_like(query)
    wide = jnp.concatenate(
        [jnp.where(first_kv, query, zero), jnp.where(first_kv, zero, query)], axis=1
    ).astype(jnp.bfloat16)
    scale = 1.0 / math.sqrt(HD)
    scores = (
        lax.dot_general(wide, keys, (((1,), (1,)), ((), ())), preferred_element_type=jnp.float32)
        * scale
    )
    span = lax.broadcasted_iota(jnp.int32, scores.shape, 1)
    scores = jnp.where(span < length * BLK, scores, -jnp.inf)
    step = lax.broadcasted_iota(jnp.int32, (32, 1), 0) // 16
    fresh = []
    for u in range(STEPS):
        key_u = jnp.where(first_kv, extra[2 * u : 2 * u + 1], extra[2 * u + 1 : 2 * u + 2])
        score_u = jnp.sum(query * key_u, axis=1, keepdims=True) * scale
        fresh.append(jnp.where(step >= u, score_u, -jnp.inf))
    top = jnp.max(scores, axis=1, keepdims=True)
    for score_u in fresh:
        top = jnp.maximum(top, score_u)
    exp_cache = jnp.exp(scores - top)
    exp_fresh = [jnp.exp(score_u - top) for score_u in fresh]
    total = jnp.sum(exp_cache, axis=1, keepdims=True)
    for exp_u in exp_fresh:
        total = total + exp_u
    weights = (exp_cache / total).astype(jnp.bfloat16)
    both = jnp.dot(weights, values, preferred_element_type=jnp.float32)
    mixed = jnp.where(first_kv, both[:, :HD], both[:, HD:])
    for u in range(STEPS):
        value_u = jnp.where(first_kv, extra[4 + 2 * u : 5 + 2 * u], extra[5 + 2 * u : 6 + 2 * u])
        weight_u = (exp_fresh[u] / total).astype(jnp.bfloat16).astype(jnp.float32)
        mixed = mixed + weight_u * value_u
    return mixed


def each(count, body):
    if count <= 8:
        for i in range(count):
            body(i)
    else:
        pl.loop(0, count)(body)


def kernel(
    G, X, R, moves, stride,
    meta, pay, perm, keys_hbm, values_hbm, weight_hbm, out,
    keys, values, weight, qsend, qrecv, att, gath, part, mixed, peer, ready, got,
    load_sem, qs, qr, zs, zr, xs, xr, ts, tr, cs, cr, fs, fr,
):
    Z = G // X
    half = R // 2
    stays = R - moves
    cols = weight.shape[1]
    me = lax.axis_index("dp")
    core = lax.axis_index("tp")
    zi, xi = me // X, me % X
    side = (core + G - me) % 2

    loads = [
        pltpu.make_async_copy(keys_hbm, keys, load_sem.at[0]),
        pltpu.make_async_copy(values_hbm, values, load_sem.at[1]),
        pltpu.make_async_copy(weight_hbm, weight, load_sem.at[2]),
    ]
    for load in loads:
        load.start()

    barrier = pltpu.get_barrier_semaphore()
    for d in range(1, G):
        pl.semaphore_signal(
            barrier, inc=1, device_id={"dp": (me + d) % G}, device_id_type=MESH
        )
    pl.semaphore_signal(barrier, inc=1, device_id={"tp": 1 - core}, device_id_type=MESH)

    for k in range(moves):
        qsend[k] = pay[meta[stays + k]]
    pl.semaphore_wait(barrier, G)

    def remote(src, dst, send, recv, target):
        return pltpu.make_async_remote_copy(
            src_ref=src, dst_ref=dst, send_sem=send, recv_sem=recv,
            device_id=target, device_id_type=MESH,
        )

    q_copies = []
    for k in range(moves):
        off = 1 + k * stride
        copy = remote(
            qsend.at[k], qrecv.at[k], qs.at[k], qr.at[k], {"dp": (me + G - off) % G}
        )
        copy.start()
        q_copies.append(copy)
    loads[0].wait()
    loads[1].wait()

    def attend_piece(p):
        for j in range(half):
            m = p * half + j
            source = pay[meta[m]] if m < stays else qrecv[m - stays]
            row = meta[m]
            att[p, pl.ds(j * 32, 32), :] = attend_slot(
                source, keys[row], values[row], meta[R + m]
            )
        for h in range(16):
            gath[p, me, :, pl.ds(h * HD, HD)] = att[
                p, pl.ds(h, 2 * half, stride=16), :
            ].astype(jnp.bfloat16)

    def z_copy(p, d):
        return remote(
            gath.at[p, me], gath.at[p, me], zs.at[p, d - 1], zr.at[p, d - 1],
            {"dp": ((zi + d) % Z) * X + xi},
        )

    def x_copy(p, dx, d):
        block = ((zi + Z - d) % Z) * X + xi
        return remote(
            gath.at[p, block], gath.at[p, block], xs.at[p, dx - 1, d], xr.at[p, dx - 1, d],
            {"dp": zi * X + (xi + dx) % X},
        )

    def send_own(p):
        for dx in range(1, X):
            x_copy(p, dx, 0).start()
        for d in range(1, Z):
            z_copy(p, d).start()

    def forward(p):
        for d in range(1, Z):
            z_copy(p, d).wait_recv()
            for dx in range(1, X):
                x_copy(p, dx, d).start()

    attend_piece(0)
    send_own(0)
    for copy in q_copies:
        copy.wait_recv()
    attend_piece(1)
    send_own(1)
    forward(0)

    def project(p):
        for dx in range(1, X):
            for d in range(Z):
                x_copy(p, dx, d).wait_recv()
        block = min(G, 8)

        def rows(b):
            lhs = gath[p, pl.ds(b * block, block)].reshape(block * 16, weight.shape[0])
            res = jnp.dot(lhs, weight[...], preferred_element_type=jnp.float32)
            part[p, pl.ds(b * block, block)] = res.reshape(block, 16, cols)

        each(G // block, rows)

        def regroup(g):
            if p == 0:
                mixed[p, g % 2, g // 2] = part[p, g]
                return
            low = lax.broadcasted_iota(jnp.int32, (8, cols), 0) // 2
            for tile in range(2):
                acc = None
                for q in range(4):
                    m = half + tile * 4 + q
                    off = 0 if m < stays else 1 + (m - stays) * stride
                    val = part[p, (g + G - off) % G, pl.ds(tile * 8, 8), :]
                    acc = val if acc is None else jnp.where(low == q, val, acc)
                mixed[p, g % 2, g // 2, pl.ds(tile * 8, 8), :] = acc

        each(G, regroup)
        t_copy(p).start()

    def t_copy(p):
        return remote(
            mixed.at[p, 1 - core], peer.at[p], ts.at[p], tr.at[p], {"tp": 1 - core}
        )

    def c_copy(p, i):
        dist = 2 * i + side
        target = (me + dist) % G
        return remote(
            ready.at[p, target // 2], got.at[p, me], cs.at[p, i], cr.at[p, dist],
            {"dp": target},
        )

    def f_copy(p, dist):
        block = (me + G - dist) % G
        return remote(
            got.at[p, block], got.at[p, block], fs.at[p, dist], fr.at[p, dist],
            {"tp": 1 - core},
        )

    def scatter(p):
        t_copy(p).wait_recv()

        def add(j):
            ready[p, j] = (mixed[p, core, j] + peer[p, j]).astype(jnp.bfloat16)

        each(G // 2, add)

        @pl.when(side == 0)
        def _():
            got[p, me] = ready[p, me // 2]
            f_copy(p, 0).start()

        @pl.when(side == 1)
        def _():
            c_copy(p, 0).start()

        for i in range(1, G // 2):
            c_copy(p, i).start()

    def collect(p):
        @pl.when(side == 0)
        def _():
            for dist in range(1, G):
                remote(
                    ready.at[p, 0], got.at[p, (me + G - dist) % G], cs.at[p, dist // 2],
                    cr.at[p, dist], {"dp": (me + dist) % G},
                ).wait_recv()
                f_copy(p, dist).start()

        @pl.when(side == 1)
        def _():
            for dist in range(G):
                block = (me + G - dist) % G
                remote(
                    got.at[p, block], got.at[p, block], fs.at[p, dist], fr.at[p, dist],
                    {"tp": 1 - core},
                ).wait_recv()

    loads[2].wait()
    project(0)
    forward(1)
    scatter(0)
    project(1)
    scatter(1)
    collect(0)
    collect(1)

    def finish(g):
        both = jnp.concatenate([got[0, g], got[1, g]], axis=0)
        res = jnp.dot(perm[...], both, preferred_element_type=jnp.float32).astype(jnp.bfloat16)
        if cols % 128 == 0:
            out[:, pl.ds(g * cols, cols)] = res
        else:
            out[g] = res

    each(G, finish)

    for copy in q_copies:
        copy.wait_send()
    for p in range(2):
        for d in range(1, Z):
            z_copy(p, d).wait_send()
        for dx in range(1, X):
            for d in range(Z):
                x_copy(p, dx, d).wait_send()
        t_copy(p).wait_send()
        for i in range(1, G // 2):
            c_copy(p, i).wait_send()

        @pl.when(side == 1)
        def _():
            c_copy(p, 0).wait_send()

        @pl.when(side == 0)
        def _():
            for dist in range(G):
                f_copy(p, dist).wait_send()


def local(cache_keys, cache_values, lengths, move_to, queries, new_keys, new_values, out_weight):
    G = lax.axis_size("dp")
    R = lengths.shape[0]
    X = 2 if G <= 16 else 4
    moves = min(R // 2, G - 1)
    stride = max(1, G // (moves + 1))
    depth, cols = out_weight.shape
    me = lax.axis_index("dp")
    ids = jnp.arange(R, dtype=jnp.int32)
    off = (move_to // R + G - me) % G
    order = jnp.where(off == 0, ids, R + off)
    rank = jnp.sum((order[None, :] < order[:, None]).astype(jnp.int32), axis=1)
    hit = rank[None, :] == ids[:, None]
    index = jnp.sum(jnp.where(hit, ids[None, :], 0), axis=1)
    length = jnp.sum(jnp.where(hit, lengths[None, :], 0), axis=1)
    meta = jnp.concatenate([index, length])
    both_ids = jnp.arange(2 * R, dtype=jnp.int32)
    home = jnp.repeat(rank, 2) * 2 + both_ids % 2
    perm = (home[:, None] == both_ids[None, :]).astype(jnp.bfloat16)
    pay = jnp.concatenate(
        [
            queries.reshape(R, 32, HD),
            new_keys.reshape(R, 4, HD),
            new_values.reshape(R, 4, HD),
            jnp.zeros((R, PAY - 40, HD), jnp.bfloat16),
        ],
        axis=1,
    )
    wide = cols % 128 == 0
    out_shape = (2 * R, G * cols) if wide else (G, 2 * R, cols)
    dma = pltpu.SemaphoreType.DMA
    Z = G // X
    vmem = pl.BlockSpec(memory_space=pltpu.VMEM)
    anywhere = pl.BlockSpec(memory_space=pl.ANY)
    result = pl.pallas_call(
        functools.partial(kernel, G, X, R, moves, stride),
        out_shape=jax.ShapeDtypeStruct(out_shape, jnp.bfloat16),
        in_specs=[pl.BlockSpec(memory_space=pltpu.SMEM), vmem, vmem, anywhere, anywhere, anywhere],
        out_specs=vmem,
        scratch_shapes=[
            pltpu.VMEM(cache_keys.shape, jnp.bfloat16),
            pltpu.VMEM(cache_values.shape, jnp.bfloat16),
            pltpu.VMEM(out_weight.shape, jnp.bfloat16),
            pltpu.VMEM((moves, PAY, HD), jnp.bfloat16),
            pltpu.VMEM((moves, PAY, HD), jnp.bfloat16),
            pltpu.VMEM((2, R * 16, HD), jnp.float32),
            pltpu.VMEM((2, G, R, depth), jnp.bfloat16),
            pltpu.VMEM((2, G, R, cols), jnp.float32),
            pltpu.VMEM((2, 2, G // 2, R, cols), jnp.float32),
            pltpu.VMEM((2, G // 2, R, cols), jnp.float32),
            pltpu.VMEM((2, G // 2, R, cols), jnp.bfloat16),
            pltpu.VMEM((2, G, R, cols), jnp.bfloat16),
            dma((3,)),
            dma((moves,)),
            dma((moves,)),
            dma((2, Z - 1)),
            dma((2, Z - 1)),
            dma((2, X - 1, Z)),
            dma((2, X - 1, Z)),
            dma((2,)),
            dma((2,)),
            dma((2, G // 2)),
            dma((2, G)),
            dma((2, G)),
            dma((2, G)),
        ],
        compiler_params=pltpu.CompilerParams(
            collective_id=0, has_side_effects=True, vmem_limit_bytes=48 * 1024 * 1024
        ),
    )(meta, pay, perm, cache_keys, cache_values, out_weight)
    if not wide:
        result = jnp.transpose(result, (1, 0, 2))
    return result.reshape(R, STEPS, G * cols)


def solution(mesh):
    placed = (
        P(("parts", "dp"), None, "tp"),
        P(("parts", "dp"), None, "tp"),
        P(("parts", "dp")),
        P(("parts", "dp")),
        P(("parts", "dp"), None, "tp"),
        P(("parts", "dp"), None, "tp"),
        P(("parts", "dp"), None, "tp"),
        P("tp", "dp"),
    )
    return jax.shard_map(
        local, mesh=mesh, in_specs=placed, out_specs=P(("parts", "dp"), None, None), check_vma=False
    )
```

time: 196 us -> 44.4 us (0.23); the launches traced: 193 us -> 44 us
  waiting for transfers between devices: 60.9 us -> 0 us
  between operations: 40.6 us -> 0.05 us
  Pallas kernels: 0 us -> 35.4 us
  blocking collectives: 28.6 us -> 0 us
  local copies, waits for them, and re-layouts: 29.5 us -> 6.74 us
  starting transfers between devices: 21.2 us -> 0 us
  matrix products: 9.67 us -> 0 us
    all_gather x1 -> x0, waiting for transfers between devices: 44.6 us -> none  [local(): lax.all_gather(flat_rows, 'dp', axis=0, tiled=True)]
    pallas_call x0 -> x1, Pallas kernels: none -> 35.4 us  [local(): pl.pallas_call(functools.partial(kernel, G, X, R, moves, stride), out_sha...]
    ppermute x14 -> x0, starting transfers between devices: 21.2 us -> none  [shifted(): lax.ppermute(shard, axis, [(i, (i + by) % count) for i in range(count)])]
    ppermute x14 -> x0, waiting for transfers between devices: 16.3 us -> none  [shifted(): lax.ppermute(shard, axis, [(i, (i + by) % count) for i in range(count)])]
    all_to_all x1 -> x0, blocking collectives: 12.7 us -> none  [local(): lax.all_to_all(summed, 'dp', split_axis=0, concat_axis=1, tiled=True)]
    dot_general x5 -> x0, matrix products: 9.67 us -> none  [the longest x1 3.06 us: local(): jnp.dot(lax.all_gather(flat_rows, 'dp', axis=0, tiled=True), out_weight,...]
    unnamed x1 -> x0, blocking collectives: 8.41 us -> none
    dynamic_update_slice x11 -> x0, local copies, waits for them, and re-layouts: 8.2 us -> none  [place_row(): return lax.dynamic_update_slice_in_dim(array, row, index, 0)]
  transfers between devices with their start and end apart: 15 -> 0, of which waited for: 4 -> 0; matrix products, arithmetic and copies ran while one was open for 9% -> 0% of each run, Pallas kernels for 0% -> 0%
where the time goes in v1:
time: 44.4 us; the launch traced here: 44 us
  Pallas kernels  35.4 us (80%)
  local copies, waits for them, and re-layouts  6.74 us (15%)
  other arithmetic  1.9 us (4%)
    pallas_call x1, Pallas kernels, local(): pl.pallas_call(functools.partial(kernel, G, X, R, moves, stride), out_sha...  35.4 us
    unnamed x4, local copies, waits for them, and re-layouts  3.18 us
    reshape x1, local copies, waits for them, and re-layouts, local(): queries.reshape(R, 32, HD)  1 us

profile of v1, /device:TPU:1, one launch (start us, length us, event | category | flops | bytes accessed | tf_op | source)
XLA Modules:
  0.0 44.0 jit_solution(11649010696638882712)
XLA Ops:
  0.0 0.7 %compare_select_fusion.2 = s32[16]{0:T(128)S(1)} fusion(s32[16]{0:T(128)} %param.11, s32[]{:T(128)S(6)} %axis_index.15), kind=kLoop, calls=%fused_computation.10 | loop fusion | flops 496 | bytes 132 | tf_op jit(solution)/shard_map/jit(_where)/select_n | solution.py:304
  0.7 0.2 convert_reduce_fusion
  0.9 0.1 pad.3.clone
  0.9 0.8 %select_reduce_fusion.1 = (s32[16]{0:T(128)S(1)}, s32[16]{0:T(128)S(1)}) fusion(s32[16]{0:T(128)S(1)} %convert_reduce_fusion, s32[16]{0:T(128)} %param.10), kind=kLoop, calls=%fused_computation.4 | loop fusion | flops 1248 | bytes 256 | tf_op jit(solution)/shard_map/reduce_sum | solution.py:307
  1.7 0.1 pad_add_fusion.meta
  1.8 0.1 broadcast_in_dim.36
  1.9 0.1 mul.18
  2.0 0.1 fusion.perm
  2.0 0.7 %reshape.35 = bf16[16,4,128]{2,1,0:T(4,128)(2,1)S(1)} reshape(bf16[16,2,256]{2,1,0:T(2,128)(2,1)} %param.13) | data formatting | bytes 32768 | tf_op jit(solution)/shard_map/reshape | solution.py:316
  2.8 0.7 %reshape.36 = bf16[16,4,128]{2,1,0:T(4,128)(2,1)S(1)} reshape(bf16[16,2,256]{2,1,0:T(2,128)(2,1)} %param.14) | data formatting | bytes 32768 | tf_op jit(solution)/shard_map/reshape | solution.py:317
  3.5 1.0 %reshape.34 = bf16[16,32,128]{2,1,0:T(8,128)(2,1)S(1)} reshape(bf16[16,2,2048]{2,1,0:T(2,128)(2,1)} %param.12) | data formatting | bytes 262144 | tf_op jit(solution)/shard_map/reshape | solution.py:315
  4.5 0.1 maximum_maximum_fusion.pay
  4.6 0.0 copy-start
  4.6 1.6 %copy-done = bf16[16,256,256]{2,1,0:T(8,128)(2,1)S(1)} copy-done((bf16[16,256,256]{2,1,0:T(8,128)(2,1)S(1)}, bf16[16,256,256]{2,1,0:T(8,128)(2,1)}, u32[]{:S(2)}) %copy-start) | copy-done | bytes 2097176
  6.2 0.0 copy-start.1
  6.2 1.6 %copy-done.1 = bf16[16,256,256]{2,1,0:T(8,128)(2,1)S(1)} copy-done((bf16[16,256,256]{2,1,0:T(8,128)(2,1)S(1)}, bf16[16,256,256]{2,1,0:T(8,128)(2,1)}, u32[]{:S(2)}) %copy-start.1) | copy-done | bytes 2097176
  7.8 35.4 %shard_map.82 = bf16[32,5120]{1,0:T(8,128)(2,1)S(1)} custom-call(s32[32]{0:T(128)S(1)} %pad_add_fusion.meta, bf16[16,48,128]{2,1,0:T(8,128)(2,1)S(1)} %maximum_maximum_fusion.pay, bf16[32,32]{1,0:T(8,128)(2,1)S(1)} %fusion.perm, bf16[16,256,256]{2,1,0:T(8,128)(2,1)S(1)} %copy-done, bf16[16,256,256]{2,1,0:T(8,128)(2,1)S(1)} %copy-done.1, ...), custom_call_target="tpu_custom_call" | custom-call | tf_op jit(solution)/shard_map/pallas_call | solution.py:328
  43.2 0.8 %reshape.37 = bf16[16,2,5120]{2,1,0:T(2,128)(2,1)} reshape(bf16[32,5120]{1,0:T(8,128)(2,1)S(1)} %shard_map.82) | data formatting | bytes 655360 | tf_op jit(solution)/shard_map/reshape | solution.py:366
  (3 shorter events, 0.0 us)
Async XLA Ops:
  4.6 1.6 %copy-start = (bf16[16,256,256]{2,1,0:T(8,128)(2,1)S(1)}, bf16[16,256,256]{2,1,0:T(8,128)(2,1)}, u32[]{:S(2)}) copy-start(bf16[16,256,256]{2,1,0:T(8,128)(2,1)} %keys_hbm.1) | copy-start | bytes 6291460
  6.2 1.6 %copy-start.1 = (bf16[16,256,256]{2,1,0:T(8,128)(2,1)S(1)}, bf16[16,256,256]{2,1,0:T(8,128)(2,1)}, u32[]{:S(2)}) copy-start(bf16[16,256,256]{2,1,0:T(8,128)(2,1)} %values_hbm.1) | copy-start | bytes 6291460

commit v2 on v1

--- a/solution.py
+++ b/solution.py
@@ -16,9 +16,7 @@
 MESH = pl.DeviceIdType.MESH
 
 
-def attend_slot(pay, keys, values, length):
-    query = pay[0:32].astype(jnp.float32)
-    extra = pay[32:48].astype(jnp.float32)
+def attend_slot(query, extra, keys, values, length):
     row = lax.broadcasted_iota(jnp.int32, (32, HD), 0)
     first_kv = (row // 8) % 2 == 0
     zero = jnp.zeros_like(query)
@@ -35,7 +33,7 @@
     step = lax.broadcasted_iota(jnp.int32, (32, 1), 0) // 16
     fresh = []
     for u in range(STEPS):
-        key_u = jnp.where(first_kv, extra[2 * u : 2 * u + 1], extra[2 * u + 1 : 2 * u + 2])
+        key_u = jnp.where(first_kv, extra[u : u + 1], extra[2 + u : 3 + u])
         score_u = jnp.sum(query * key_u, axis=1, keepdims=True) * scale
         fresh.append(jnp.where(step >= u, score_u, -jnp.inf))
     top = jnp.max(scores, axis=1, keepdims=True)
@@ -50,10 +48,14 @@
     both = jnp.dot(weights, values, preferred_element_type=jnp.float32)
     mixed = jnp.where(first_kv, both[:, :HD], both[:, HD:])
     for u in range(STEPS):
-        value_u = jnp.where(first_kv, extra[4 + 2 * u : 5 + 2 * u], extra[5 + 2 * u : 6 + 2 * u])
+        value_u = jnp.where(first_kv, extra[4 + u : 5 + u], extra[6 + u : 7 + u])
         weight_u = (exp_fresh[u] / total).astype(jnp.bfloat16).astype(jnp.float32)
         mixed = mixed + weight_u * value_u
     return mixed
+
+
+def equal(a, b):
+    return 1 - jnp.minimum(jnp.maximum(a - b, b - a), 1)
 
 
 def each(count, body):
@@ -66,8 +68,8 @@
 
 def kernel(
     G, X, R, moves, stride,
-    meta, pay, perm, keys_hbm, values_hbm, weight_hbm, out,
-    keys, values, weight, qsend, qrecv, att, gath, part, mixed, peer, ready, got,
+    move_to, lengths, queries, new_keys, new_values, keys_hbm, values_hbm, weight_hbm, out,
+    keys, values, weight, qall, qrow, qsend, qrecv, att, gath, part, mixed, peer, ready, got,
     load_sem, qs, qr, zs, zr, xs, xr, ts, tr, cs, cr, fs, fr,
 ):
     Z = G // X
@@ -94,8 +96,38 @@
         )
     pl.semaphore_signal(barrier, inc=1, device_id={"tp": 1 - core}, device_id_type=MESH)
 
+    offs = [lax.rem(lax.div(move_to[i], R) + G - me, G) for i in range(R)]
+    index = [jnp.int32(0)] * R
+    seen = jnp.int32(0)
+    for i in range(R):
+        leaves = jnp.minimum(offs[i], 1)
+        slot = (1 - leaves) * seen + leaves * (stays + lax.div(offs[i] + stride - 1, stride) - 1)
+        seen = seen + 1 - leaves
+        index = [index[m] + i * equal(slot, m) for m in range(R)]
+    index = [jnp.minimum(row, R - 1) for row in index]
+
+    flat = queries[...].astype(jnp.float32).reshape(2 * R, 16 * HD)
+    for h in range(16):
+        qall[pl.ds(h, 2 * R, stride=16), :] = flat[:, h * HD : (h + 1) * HD]
+    for i in range(R):
+        qrow[i] = qall[i * 32 : i * 32 + 32, :].astype(jnp.bfloat16)
+
+    def own_query(row):
+        return qrow[row].astype(jnp.float32)
+
+    def own_extra(row):
+        key = new_keys[row].astype(jnp.float32)
+        value = new_values[row].astype(jnp.float32)
+        return jnp.concatenate(
+            [key[:, :HD], key[:, HD:], value[:, :HD], value[:, HD:]], axis=0
+        )
+
     for k in range(moves):
-        qsend[k] = pay[meta[stays + k]]
+        row = index[stays + k]
+        qsend[k, 0:32] = qrow[row]
+        qsend[k, 32:48] = jnp.concatenate(
+            [own_extra(row), jnp.zeros((8, HD), jnp.float32)], axis=0
+        ).astype(jnp.bfloat16)
     pl.semaphore_wait(barrier, G)
 
     def remote(src, dst, send, recv, target):
@@ -118,10 +150,14 @@
     def attend_piece(p):
         for j in range(half):
             m = p * half + j
-            source = pay[meta[m]] if m < stays else qrecv[m - stays]
-            row = meta[m]
+            row = index[m]
+            if m < stays:
+                query, extra = own_query(row), own_extra(row)
+            else:
+                query = qrecv[m - stays, 0:32].astype(jnp.float32)
+                extra = qrecv[m - stays, 32:48].astype(jnp.float32)
             att[p, pl.ds(j * 32, 32), :] = attend_slot(
-                source, keys[row], values[row], meta[R + m]
+                query, extra, keys[row], values[row], lengths[row]
             )
         for h in range(16):
             gath[p, me, :, pl.ds(h * HD, HD)] = att[
@@ -147,8 +183,8 @@
         for d in range(1, Z):
             z_copy(p, d).start()
 
-    def forward(p):
-        for d in range(1, Z):
+    def forward(p, first, last):
+        for d in range(first, last):
             z_copy(p, d).wait_recv()
             for dx in range(1, X):
                 x_copy(p, dx, d).start()
@@ -159,7 +195,8 @@
         copy.wait_recv()
     attend_piece(1)
     send_own(1)
-    forward(0)
+    forward(0, 1, Z)
+    forward(1, 1, Z // 2)
 
     def project(p):
         for dx in range(1, X):
@@ -252,20 +289,27 @@
 
     loads[2].wait()
     project(0)
-    forward(1)
+    forward(1, Z // 2, Z)
     scatter(0)
     project(1)
     scatter(1)
     collect(0)
     collect(1)
 
+    to_row = lax.broadcasted_iota(jnp.int32, (2 * R, 2 * R), 0)
+    from_row = lax.broadcasted_iota(jnp.int32, (2 * R, 2 * R), 1)
+    held = jnp.zeros((2 * R, 2 * R), jnp.int32)
+    for m in range(R):
+        held = jnp.where(from_row // 2 == m, index[m], held)
+    perm = equal(held * 2 + from_row % 2, to_row).astype(jnp.float32).astype(jnp.bfloat16)
+
     def finish(g):
         both = jnp.concatenate([got[0, g], got[1, g]], axis=0)
-        res = jnp.dot(perm[...], both, preferred_element_type=jnp.float32).astype(jnp.bfloat16)
+        res = jnp.dot(perm, both, preferred_element_type=jnp.float32)
         if cols % 128 == 0:
-            out[:, pl.ds(g * cols, cols)] = res
+            out[:, :, pl.ds(g * cols, cols)] = res.reshape(R, STEPS, cols).astype(jnp.bfloat16)
         else:
-            out[g] = res
+            out[g] = res.astype(jnp.bfloat16)
 
     each(G, finish)
 
@@ -298,42 +342,24 @@
     moves = min(R // 2, G - 1)
     stride = max(1, G // (moves + 1))
     depth, cols = out_weight.shape
-    me = lax.axis_index("dp")
-    ids = jnp.arange(R, dtype=jnp.int32)
-    off = (move_to // R + G - me) % G
-    order = jnp.where(off == 0, ids, R + off)
-    rank = jnp.sum((order[None, :] < order[:, None]).astype(jnp.int32), axis=1)
-    hit = rank[None, :] == ids[:, None]
-    index = jnp.sum(jnp.where(hit, ids[None, :], 0), axis=1)
-    length = jnp.sum(jnp.where(hit, lengths[None, :], 0), axis=1)
-    meta = jnp.concatenate([index, length])
-    both_ids = jnp.arange(2 * R, dtype=jnp.int32)
-    home = jnp.repeat(rank, 2) * 2 + both_ids % 2
-    perm = (home[:, None] == both_ids[None, :]).astype(jnp.bfloat16)
-    pay = jnp.concatenate(
-        [
-            queries.reshape(R, 32, HD),
-            new_keys.reshape(R, 4, HD),
-            new_values.reshape(R, 4, HD),
-            jnp.zeros((R, PAY - 40, HD), jnp.bfloat16),
-        ],
-        axis=1,
-    )
     wide = cols % 128 == 0
-    out_shape = (2 * R, G * cols) if wide else (G, 2 * R, cols)
+    out_shape = (R, STEPS, G * cols) if wide else (G, 2 * R, cols)
     dma = pltpu.SemaphoreType.DMA
     Z = G // X
+    smem = pl.BlockSpec(memory_space=pltpu.SMEM)
     vmem = pl.BlockSpec(memory_space=pltpu.VMEM)
     anywhere = pl.BlockSpec(memory_space=pl.ANY)
     result = pl.pallas_call(
         functools.partial(kernel, G, X, R, moves, stride),
         out_shape=jax.ShapeDtypeStruct(out_shape, jnp.bfloat16),
-        in_specs=[pl.BlockSpec(memory_space=pltpu.SMEM), vmem, vmem, anywhere, anywhere, anywhere],
+        in_specs=[smem, smem, vmem, vmem, vmem, anywhere, anywhere, anywhere],
         out_specs=vmem,
         scratch_shapes=[
             pltpu.VMEM(cache_keys.shape, jnp.bfloat16),
             pltpu.VMEM(cache_values.shape, jnp.bfloat16),
             pltpu.VMEM(out_weight.shape, jnp.bfloat16),
+            pltpu.VMEM((R * 32, HD), jnp.float32),
+            pltpu.VMEM((R, 32, HD), jnp.bfloat16),
             pltpu.VMEM((moves, PAY, HD), jnp.bfloat16),
             pltpu.VMEM((moves, PAY, HD), jnp.bfloat16),
             pltpu.VMEM((2, R * 16, HD), jnp.float32),
@@ -358,12 +384,12 @@
             dma((2, G)),
         ],
         compiler_params=pltpu.CompilerParams(
-            collective_id=0, has_side_effects=True, vmem_limit_bytes=48 * 1024 * 1024
+            collective_id=0, has_side_effects=True, vmem_limit_bytes=60 * 1024 * 1024
         ),
-    )(meta, pay, perm, cache_keys, cache_values, out_weight)
-    if not wide:
-        result = jnp.transpose(result, (1, 0, 2))
-    return result.reshape(R, STEPS, G * cols)
+    )(move_to, lengths, queries, new_keys, new_values, cache_keys, cache_values, out_weight)
+    if wide:
+        return result
+    return jnp.transpose(result, (1, 0, 2)).reshape(R, STEPS, G * cols)
 
 
 def solution(mesh):

time: 44.4 us -> 37.8 us (0.85)
  local copies, waits for them, and re-layouts: 6.74 us -> 1.92 us
  other arithmetic: 1.9 us -> 0 us
    reshape x4 -> x0, local copies, waits for them, and re-layouts: 3.32 us -> none  [the longest x1 1 us: local(): queries.reshape(R, 32, HD)]
    unnamed x4 -> x1, local copies, waits for them, and re-layouts: 3.18 us -> 1.92 us
    reduce_sum x2 -> x0, other arithmetic: 0.95 us -> none  [the longest x1 0.77 us: local(): index = jnp.sum(jnp.where(hit, ids[None, :], 0), axis=1)]
    select_n x1 -> x0, other arithmetic: 0.67 us -> none  [local(): order = jnp.where(off == 0, ids, R + off)]
where the time goes in v2:
time: 37.8 us; the launch traced here: 37.7 us
  Pallas kernels  35.7 us (94%)
  local copies, waits for them, and re-layouts  1.92 us (5%)
    pallas_call x1, Pallas kernels, local(): pl.pallas_call(functools.partial(kernel, G, X, R, moves, stride), out_sha...  35.7 us
    unnamed x1, local copies, waits for them, and re-layouts  1.92 us

profile of v2, /device:TPU:1, one launch (start us, length us, event | category | flops | bytes accessed | tf_op | source)
XLA Modules:
  0.0 37.7 jit_solution(2095305959267871656)
XLA Ops:
  0.0 35.7 %shard_map.82 = bf16[16,2,5120]{2,1,0:T(2,128)(2,1)} custom-call(s32[16]{0:T(128)} %move_to.1, s32[16]{0:T(128)} %lengths.1, bf16[16,2,2048]{2,1,0:T(2,128)(2,1)} %queries.1, bf16[16,2,256]{2,1,0:T(2,128)(2,1)} %new_keys.1, bf16[16,2,256]{2,1,0:T(2,128)(2,1)} %new_values.1, bf16[16,256,256]{2,1,0:T(8,128)(2,1)} %keys_hbm.1, ...), custom_call_target="tpu_custom_call" | custom-call | tf_op jit(solution)/shard_map/pallas_call | solution.py:352
  35.7 1.9 %copy.10 = bf16[16,2,5120]{2,1,0:T(2,128)(2,1)} copy(bf16[16,2,5120]{2,1,0:T(2,128)(2,1)} %shard_map.82) | data formatting | bytes 655360

commit v3 on v2

--- a/solution.py
+++ b/solution.py
@@ -178,9 +178,10 @@
         )
 
     def send_own(p):
+        z_copy(p, 1).start()
         for dx in range(1, X):
             x_copy(p, dx, 0).start()
-        for d in range(1, Z):
+        for d in range(2, Z):
             z_copy(p, d).start()
 
     def forward(p, first, last):
@@ -196,7 +197,7 @@
     attend_piece(1)
     send_own(1)
     forward(0, 1, Z)
-    forward(1, 1, Z // 2)
+    forward(1, 1, Z)
 
     def project(p):
         for dx in range(1, X):
@@ -289,7 +290,6 @@
 
     loads[2].wait()
     project(0)
-    forward(1, Z // 2, Z)
     scatter(0)
     project(1)
     scatter(1)

time: 37.8 us -> 37.4 us (0.989)
  Pallas kernels: 35.7 us -> 35.3 us
    pallas_call x1, Pallas kernels: 35.7 us -> 35.3 us  [local(): pl.pallas_call(functools.partial(kernel, G, X, R, moves, stride), out_sha...]
where the time goes in v3:
time: 37.4 us; the launch traced here: 37.3 us
  Pallas kernels  35.3 us (94%)
  local copies, waits for them, and re-layouts  1.92 us (5%)
    pallas_call x1, Pallas kernels, local(): pl.pallas_call(functools.partial(kernel, G, X, R, moves, stride), out_sha...  35.3 us
    unnamed x1, local copies, waits for them, and re-layouts  1.92 us

profile of v3, /device:TPU:1, one launch (start us, length us, event | category | flops | bytes accessed | tf_op | source)
XLA Modules:
  0.0 37.3 jit_solution(16644413945410377519)
XLA Ops:
  0.0 35.3 %shard_map.82 = bf16[16,2,5120]{2,1,0:T(2,128)(2,1)} custom-call(s32[16]{0:T(128)} %move_to.1, s32[16]{0:T(128)} %lengths.1, bf16[16,2,2048]{2,1,0:T(2,128)(2,1)} %queries.1, bf16[16,2,256]{2,1,0:T(2,128)(2,1)} %new_keys.1, bf16[16,2,256]{2,1,0:T(2,128)(2,1)} %new_values.1, bf16[16,256,256]{2,1,0:T(8,128)(2,1)} %keys_hbm.1, ...), custom_call_target="tpu_custom_call" | custom-call | tf_op jit(solution)/shard_map/pallas_call | solution.py:352
  35.3 1.9 %copy.10 = bf16[16,2,5120]{2,1,0:T(2,128)(2,1)} copy(bf16[16,2,5120]{2,1,0:T(2,128)(2,1)} %shard_map.82) | data formatting | bytes 655360
